TPU v7x, 32 devices: a whole 2x2x4 slice. The times are simulated.
32 devices in a mesh: gx: 8 (over z, y), gz: 4 (over x, core).
Axes of the slice: x: 2, y: 2, z: 4, core: 2. Of those that a mesh axis runs over, the one named last changes fastest.
Arguments:
- whitened: float32 [2, 64, 1024, 512], P(None, 'gz', 'gx'), may hold values from -6 to 6
- observed: float32 [2, 1024, 512], P(None, 'gx'), may hold values from -12 to 12
- lower_x: bfloat16 [1024, 1024], P('gx'), as said below
- lower_y: bfloat16 [512, 512], P('gx'), as said below
- lower_z: bfloat16 [64, 64], replicated, as said below
- coupling_kernel: float32 [2, 3, 3, 3], replicated, may hold values from -1.25 to 1.25
Outputs:
- gradient: float32 [2, 64, 1024, 512], P(None, 'gz', 'gx')
- misfit: float32 [2, 1024, 512], P(None, 'gx')
Inputs may be any that keep to these rules, and one draw needn't show every extreme that they name: `lower_x`: lower triangular: zero above the diagonal, diagonal entries between 0.5 and 1.5. `lower_y`: lower triangular: zero above the diagonal, diagonal entries between 0.5 and 1.5. `lower_z`: lower triangular: zero above the diagonal, diagonal entries between 0.5 and 1.5.
All inputs are finite; a program needn't handle non-finite values.
Results may differ from a plain program's by a relative error of at most 0.013.
The roundings to bfloat16 on the way count: a program that leaves them out, or rounds other values in their place, can miss the bound.
Values may be sent and summed in bfloat16 or wider, within the bound.
A program may use at most 128 MiB of HBM per device.

v0:
```python
import math
import jax
import jax.numpy as jnp
from jax import lax
from jax.sharding import PartitionSpec as P

NZ = 64


def padded_2(x, sides, width):
    for axis, dim in sides:
        peers, length = (lax.axis_size(axis), x.shape[dim])
        up = [(i, (i + 1) % peers) for i in range(peers - 1)]
        down = [(j, i) for i, j in up]
        last = lax.slice_in_dim(x, length - width, length, axis=dim)
        first = lax.slice_in_dim(x, 0, width, axis=dim)
        before = lax.ppermute(last, axis, up)
        after = lax.ppermute(first, axis, down)
        x = jnp.concatenate([before, x, after], axis=dim)
    return x


def depth_lines(values, local_step):
    turned = lax.all_to_all(values, "gz", split_axis=3, concat_axis=1, tiled=True)
    return lax.all_to_all(local_step(turned), "gz", split_axis=1, concat_axis=3, tiled=True)


def across_lines(values, local_step):
    turned = lax.all_to_all(values, "gx", split_axis=3, concat_axis=2, tiled=True)
    return lax.all_to_all(local_step(turned), "gx", split_axis=2, concat_axis=3, tiled=True)


def stencil_sum(padded, kernel, depth_rows, x_rows, y_rows, flipped):
    total = jnp.zeros(padded.shape[:-3] + (depth_rows, x_rows, y_rows), jnp.float32)
    for offset_z in range(3):
        for offset_x in range(3):
            for offset_y in range(3):
                start_z = 2 - offset_z if flipped else offset_z
                start_x = 2 - offset_x if flipped else offset_x
                start_y = 2 - offset_y if flipped else offset_y
                total = (
                    total
                    + kernel[offset_z, offset_x, offset_y]
                    * padded[
                        ...,
                        start_z : start_z + depth_rows,
                        start_x : start_x + x_rows,
                        start_y : start_y + y_rows,
                    ]
                )
    return total


def depth_weights(first_row, depth_rows):
    depth = (first_row + jnp.arange(depth_rows)).astype(jnp.float32)
    factor = 4.0 / math.sqrt(NZ)
    return (factor / (1.0 + depth / NZ) ** 2, factor / (1.0 + depth / NZ) ** 3)


def coupling_forward(rim, magnetic_f, kernel, shape):
    depth_rows, x_rows, y_rows = shape
    pre_scale = stencil_sum(rim, kernel[0], depth_rows, x_rows, y_rows, False)
    pre_shift = stencil_sum(rim, kernel[1], depth_rows, x_rows, y_rows, False)
    scale = jnp.tanh(pre_scale)
    growth = jnp.exp(scale)
    return (scale, growth, magnetic_f * growth + pre_shift)


def local(whitened, observed, lower_x, lower_y, lower_z, coupling_kernel):
    factor_x, factor_y = (
        lax.all_gather(lower_x, "gx", axis=0, tiled=True),
        lax.all_gather(lower_y, "gx", axis=0, tiled=True),
    )

    def apply_depth(values):
        return jnp.einsum(
            "zk,fkxy->fzxy", lower_z, values, preferred_element_type=jnp.float32
        ).astype(jnp.bfloat16)

    def apply_across(values):
        return jnp.einsum(
            "xk,fzky->fzxy", factor_x, values, preferred_element_type=jnp.float32
        ).astype(jnp.bfloat16)

    def depth_adjoint(values):
        return jnp.einsum(
            "kz,fkxy->fzxy", lower_z, values, preferred_element_type=jnp.float32
        ).astype(jnp.bfloat16)

    def across_adjoint(values):
        return jnp.einsum(
            "kx,fzky->fzxy", factor_x, values, preferred_element_type=jnp.float32
        ).astype(jnp.bfloat16)

    start = whitened.astype(jnp.bfloat16)
    first = jnp.einsum("fzxk,yk->fzxy", start, factor_y, preferred_element_type=jnp.float32).astype(
        jnp.bfloat16
    )
    model = across_lines(depth_lines(first, apply_depth), apply_across)
    density = model[0]
    magnetic_f = model[1].astype(jnp.float32)
    depth_rows, x_rows, y_rows = density.shape
    rim = padded_2(density, (("gx", 1), ("gz", 0)), 1)
    rim = jnp.pad(rim, ((0, 0), (0, 0), (1, 1))).astype(jnp.float32)
    scale, growth, coupled = coupling_forward(
        rim, magnetic_f, coupling_kernel, (depth_rows, x_rows, y_rows)
    )
    weight_g, weight_m = depth_weights(lax.axis_index("gz") * depth_rows, depth_rows)
    part_g = jnp.einsum("z,zxy->xy", weight_g, density.astype(jnp.float32))
    part_m = jnp.einsum("z,zxy->xy", weight_m, coupled)
    predicted = lax.psum(jnp.stack([part_g, part_m]), "gz")
    misfit = predicted - observed
    back_g = weight_g[:, None, None] * misfit[0][None]
    back_m = weight_m[:, None, None] * misfit[1][None]
    back_scale = (back_m * magnetic_f * growth * (1.0 - scale * scale)).astype(jnp.bfloat16)
    back_shift = back_m.astype(jnp.bfloat16)
    cotangents = jnp.stack([back_scale, back_shift])
    outer = padded_2(cotangents, (("gx", 2), ("gz", 1)), 1)
    outer = jnp.pad(outer, ((0, 0), (0, 0), (0, 0), (1, 1))).astype(jnp.float32)
    spread_back = stencil_sum(outer[0], coupling_kernel[0], depth_rows, x_rows, y_rows, True)
    spread_back = spread_back + stencil_sum(
        outer[1], coupling_kernel[1], depth_rows, x_rows, y_rows, True
    )
    adjoint = jnp.stack([back_g + spread_back, back_m * growth]).astype(jnp.bfloat16)
    fourth = depth_lines(across_lines(adjoint, across_adjoint), depth_adjoint)
    gradient = whitened + jnp.einsum(
        "fzxk,ky->fzxy", fourth, factor_y, preferred_element_type=jnp.float32
    )
    return (gradient, misfit)


def solution(mesh):
    in_specs = (
        P(None, "gz", "gx", None),
        P(None, "gx", None),
        P("gx", None),
        P("gx", None),
        P(),
        P(),
    )
    out_specs = (P(None, "gz", "gx", None), P(None, "gx", None))
    return jax.shard_map(local, mesh=mesh, in_specs=in_specs, out_specs=out_specs, check_vma=False)
```

profile of v0, /device:TPU:0, one launch (start us, length us, event | category | flops | bytes accessed | tf_op | source)
XLA Modules:
  0.0 1367.9 jit_solution(581240853023325873)
XLA Ops:
  7.2 33.2 %all_gather.6 = bf16[512,512]{1,0:T(8,128)(2,1)S(1)} all-gather(bf16[64,512]{1,0:T(8,128)(2,1)} %param.9), channel_id=1, replica_groups=mesh['gx'=8,'gz'=4] {'gx'}, dimensions={0}, use_global_device_ids=true | all-gather | bytes 589824 | tf_op jit(solution)/shard_map/all_gather | solution.py:72
  41.2 7.8 fusion.77
  49.0 7.9 copy.51
  56.9 53.9 %all_to_all.141 = bf16[2,16,128,512]{2,1,0,3:T(8,128)(2,1)} all-to-all(bf16[2,16,128,512]{2,1,0,3:T(8,128)(2,1)} %copy.51), channel_id=1, replica_groups=mesh['gx'=8,'gz'=4] {'gz'}, dimensions={3} | all-to-all | bytes 8388608 | tf_op jit(solution)/shard_map/all_to_all | solution.py:24
  110.7 9.0 copy.52
  125.8 51.6 %all_to_all.142 = bf16[2,64,128,128]{3,2,0,1:T(8,128)(2,1)} all-to-all(bf16[2,64,128,128]{3,2,0,1:T(8,128)(2,1)S(1)} %copy.53), channel_id=1, replica_groups=mesh['gx'=8,'gz'=4] {'gz'}, dimensions={1} | all-to-all | bytes 8388608 | tf_op jit(solution)/shard_map/all_to_all | solution.py:25
  177.4 7.8 copy.95
  191.7 117.5 %all-to-all-done.2 = bf16[2,16,128,512]{2,1,0,3:T(8,128)(2,1)} async-done(((bf16[2,16,128,512]{2,1,0,3:T(8,128)(2,1)}), bf16[2,16,128,512]{2,1,0,3:T(8,128)(2,1)}, u32[]{:S(2)}, u32[]{:S(2)}) %all-to-all-start.2) | async-done | bytes 4194336 | tf_op jit(solution)/shard_map/all_to_all | solution.py:29
  316.1 7.3 all_to_all.113
  323.4 9.5 convert_bitcast_fusion.2
  332.8 12.9 copy.59
  345.7 10.5 reshape.38
  363.3 90.1 %all-to-all-done.3 = bf16[8,2,131072]{2,1,0:T(2,128)(2,1)} async-done(((bf16[8,2,131072]{2,1,0:T(2,128)(2,1)}), bf16[8,2,131072]{2,1,0:T(2,128)(2,1)}, u32[]{:S(2)}, u32[]{:S(2)}) %all-to-all-start.3) | async-done | bytes 4194336 | tf_op jit(solution)/shard_map/all_to_all | solution.py:30
  453.4 10.3 reshape.39
  463.7 9.3 copy.97
  506.6 11.2 fusion.10
  517.8 122.0 %add_add_fusion = (bf16[16,128,512]{1,2,0:T(8,128)(2,1)S(1)}, f32[16,128,512]{1,2,0:T(8,128)}) fusion(f32[16,128,512]{1,2,0:T(8,128)} %bitcast.166, f32[18,130,514]{1,2,0:T(8,128)} %fusion.10, f32[]{:T(128)} %bitcast.79, f32[]{:T(128)} %bitcast.78, f32[]{:T(128)} %bitcast.77, f32[]{:T(128)} %bitcast.76, f32[]{:T(128)} %bitcast.75, f32[]{:T(128)} %bitcast.74, ...), kind=kLoop, calls=%fused_computation.148 | loop fusion | flops 114294784 | bytes 123732184 | tf_op jit(solution)/shard_map/add | solution.py:66
  645.7 35.0 %all-reduce.4.cloned.1.call-done = f32[2,128,512]{2,1,0:T(8,128)} async-done(((f32[2,128,512]{2,1,0:T(8,128)}), f32[2,128,512]{2,1,0:T(8,128)}) %all-reduce.4.cloned.1.call-update) | async-done | bytes 524304 | tf_op jit(solution)/shard_map/psum | solution.py:111
  723.4 22.6 %fusion.1 = f32[2,18,130,514]{2,3,1,0:T(8,128)S(1)} fusion(bf16[2,1,130,512]{2,3,1,0:T(8,128)(2,1)} %collective-permute-done.7, bf16[2,1,130,512]{2,3,1,0:T(8,128)(2,1)S(1)} %collective-permute-done.6, bf16[2,16,1,512]{2,3,1,0:T(8,128)(2,1)} %copy.73, bf16[2,16,1,512]{2,3,1,0:T(8,128)(2,1)} %copy.72, bf16[1,16,128,512]{2,3,1,0:T(8,128)(2,1)S(1)} %multiply_convert_fusion, ...), kind=kLoop, calls=%fused_computation.8 | loop fusion | flops 50515920 | bytes 14414400 | tf_op jit(solution)/shard_map/convert_element_type | solution.py:119
  752.9 196.9 %fusion.84 = bf16[1,16,128,512]{2,3,1,0:T(8,128)(2,1)S(1)} fusion(f32[18,130,514]{1,2,0:T(8,128)} %get-tuple-element.5, f32[]{:T(128)} %bitcast.79, f32[]{:T(128)} %bitcast.78, f32[]{:T(128)} %bitcast.77, f32[]{:T(128)} %bitcast.76, f32[]{:T(128)} %bitcast.75, f32[]{:T(128)} %bitcast.74, f32[]{:T(128)} %bitcast.73, f32[]{:T(128)} %bitcast.72, f32[]{:T(128)} %bitcast.71, ...), kind=kLoop, calls=%fused_computation.161 | loop fusion | flops 115343360 | bytes 228852000 | tf_op jit(solution)/shard_map/stack | solution.py:124
  952.9 97.5 %all_to_all.143 = bf16[2,16,128,512]{2,1,0,3:T(8,128)(2,1)S(1)} all-to-all(bf16[2,16,128,512]{2,1,0,3:T(8,128)(2,1)S(1)} %copy.74), channel_id=1, replica_groups=mesh['gx'=8,'gz'=4] {'gx'}, dimensions={3} | all-to-all | bytes 8388608 | tf_op jit(solution)/shard_map/all_to_all | solution.py:29
  1055.1 7.4 all_to_all.120
  1062.6 8.4 convert_bitcast_fusion.1
  1071.0 12.9 copy.77
  1083.9 10.5 reshape.40
  1094.3 97.9 %all_to_all.144 = bf16[8,2,131072]{2,1,0:T(2,128)(2,1)} all-to-all(bf16[8,2,131072]{2,1,0:T(2,128)(2,1)} %reshape.40), channel_id=1, replica_groups=mesh['gx'=8,'gz'=4] {'gx'}, dimensions={0} | all-to-all | bytes 8388608 | tf_op jit(solution)/shard_map/all_to_all | solution.py:30
  1192.2 10.3 reshape.41
  1202.5 14.8 %copy.101 = bf16[2,16,128,8,64]{2,1,0,4,3:T(8,128)(2,1)} copy(bf16[2,16,128,8,64]{4,1,0,2,3:T(8,128)(2,1)} %bitcast.171) | data formatting | bytes 8388608 | tf_op jit(solution)/shard_map/all_to_all | solution.py:30
  1217.2 54.1 %all_to_all.145 = bf16[2,16,128,512]{2,1,0,3:T(8,128)(2,1)} all-to-all(bf16[2,16,128,512]{2,1,0,3:T(8,128)(2,1)} %bitcast.173), channel_id=1, replica_groups=mesh['gx'=8,'gz'=4] {'gz'}, dimensions={3} | all-to-all | bytes 8388608 | tf_op jit(solution)/shard_map/all_to_all | solution.py:24
  1271.3 9.0 copy.82
  1286.5 50.7 %all_to_all.146 = bf16[2,64,128,128]{3,2,0,1:T(8,128)(2,1)S(1)} all-to-all(bf16[2,64,128,128]{3,2,0,1:T(8,128)(2,1)S(1)} %copy.84), channel_id=1, replica_groups=mesh['gx'=8,'gz'=4] {'gz'}, dimensions={1} | all-to-all | bytes 8388608 | tf_op jit(solution)/shard_map/all_to_all | solution.py:25
  1350.4 10.4 convolution_add_fusion
  (95 shorter events, 143.2 us)
Async XLA Ops:
  7.2 112.5 %copy-start = (bf16[64,64]{1,0:T(8,128)(2,1)S(1)}, bf16[64,64]{1,0:T(8,128)(2,1)}, u32[]{:S(2)}) copy-start(bf16[64,64]{1,0:T(8,128)(2,1)} %param.10) | copy-start | bytes 24580
  40.4 0.8 copy-start.7
  185.3 123.9 %all-to-all-start.2 = ((bf16[2,16,128,512]{2,1,0,3:T(8,128)(2,1)}), bf16[2,16,128,512]{2,1,0,3:T(8,128)(2,1)}, u32[]{:S(2)}, u32[]{:S(2)}) async-start(bf16[2,16,128,512]{2,1,0,3:T(8,128)(2,1)} %bitcast.174), calls=%async_computation.2 | async-start | bytes 8388608 | tf_op jit(solution)/shard_map/all_to_all | solution.py:29
  191.0 132.4 %all-gather.2.cloned.1.call-start = ((), (), s32[]{:S(2)}) async-start(), calls=%async_computation.8 | async-start | bytes 2359296 | tf_op jit(solution)/shard_map/all_gather | solution.py:71
  356.2 4.9 copy-start.11
  356.2 97.2 %all-to-all-start.3 = ((bf16[8,2,131072]{2,1,0:T(2,128)(2,1)}), bf16[8,2,131072]{2,1,0:T(2,128)(2,1)}, u32[]{:S(2)}, u32[]{:S(2)}) async-start(bf16[8,2,131072]{2,1,0:T(2,128)(2,1)} %reshape.38), calls=%async_computation.3 | async-start | bytes 8388608 | tf_op jit(solution)/shard_map/all_to_all | solution.py:30
  360.9 319.8 %all-reduce.4.cloned.1.call-start = ((), (), s32[]{:S(2)}) async-start(), calls=%async_computation.9 | async-start | bytes 1048576 | tf_op jit(solution)/shard_map/psum | solution.py:111
  485.1 11.4 collective-permute-start.1
  486.4 8.3 collective-permute-start
  498.3 4.3 copy-start.5
  498.3 4.8 copy-start.4
  499.9 6.0 collective-permute-start.2
  501.4 4.6 collective-permute-start.3
  503.1 2.8 copy-start.2
  503.2 3.4 copy-start.3
  639.8 41.0 %copy-start.10 = (f32[2,128,512]{2,1,0:T(8,128)S(1)}, f32[2,128,512]{2,1,0:T(8,128)}, u32[]{:S(2)}) copy-start(f32[2,128,512]{2,1,0:T(8,128)} %param.7) | copy-start | bytes 1572868
  681.9 0.8 copy-start.9
  689.7 4.5 copy-start.1
  697.9 8.7 collective-permute-start.4
  705.3 5.8 collective-permute-start.5
  717.2 3.0 collective-permute-start.6
  718.5 4.9 collective-permute-start.7
  752.9 196.9 %copy-start.6 = (bf16[1,16,128,512]{2,3,1,0:T(8,128)(2,1)S(1)}, bf16[1,16,128,512]{2,3,1,0:T(8,128)(2,1)}, u32[]{:S(2)}) copy-start(bf16[1,16,128,512]{2,3,1,0:T(8,128)(2,1)} %get-tuple-element.11) | copy-start | bytes 6291460
  1055.1 7.4 copy-start.12
  1343.1 7.3 copy-start.8
Sparse Core Ops, SparseCore 0:
  193.9 102.6 all-gather.1
  645.8 34.8 all-reduce.3
where the time goes:
time: 1380 us; the launch traced here: 1370 us
  blocking collectives  439 us (32%)
  other arithmetic  376 us (27%)
  waiting for transfers between devices  248 us (18%)
  local copies, waits for them, and re-layouts  219 us (16%)
  matrix products  45.4 us (3%)
  starting transfers between devices  26.9 us (2%)
  between operations  14.6 us (1%)
    another operation x2, other arithmetic, local(): jnp.stack([back_g + spread_back, back_m * growth]).astype(jnp.bfloat16)  197 us
    add x1, other arithmetic, coupling_forward(): return (scale, growth, magnetic_f * growth + pre_shift)  122 us
    all_to_all x1, waiting for transfers between devices, across_lines(): lax.all_to_all(values, 'gx', split_axis=3, concat_axis=2, tiled=True)  117 us
    all_to_all x2, blocking collectives, depth_lines(): lax.all_to_all(values, 'gz', split_axis=3, concat_axis=1, tiled=True)  108 us
    all_to_all x2, blocking collectives, depth_lines(): lax.all_to_all(local_step(turned), 'gz', split_axis=1, concat_axis=3, til...  102 us
    all_to_all x1, blocking collectives, across_lines(): lax.all_to_all(local_step(turned), 'gx', split_axis=2, concat_axis=3, til...  97.9 us
    all_to_all x1, blocking collectives, across_lines(): lax.all_to_all(values, 'gx', split_axis=3, concat_axis=2, tiled=True)  97.5 us
    all_to_all x1, waiting for transfers between devices, across_lines(): lax.all_to_all(local_step(turned), 'gx', split_axis=2, concat_axis=3, til...  90.1 us
  transfers between devices with their start and end apart: 12, of which 6 were waited for; matrix products, arithmetic and copies ran while one was open for 2% of the time, Pallas kernels for 0%

commit v1 on v0

--- a/solution.py
+++ b/solution.py
@@ -5,6 +5,22 @@
 from jax.sharding import PartitionSpec as P
 
 NZ = 64
+
+
+def swapped_with_each(x, axis, split, join):
+    ways, here = (lax.axis_size(axis), lax.axis_index(axis))
+    width = x.shape[split] // ways
+    shape = list(x.shape)
+    shape[split] = width
+    height = shape[join]
+    shape[join] = height * ways
+    full = jnp.zeros(shape, x.dtype)
+    for mask in range(ways):
+        part = lax.dynamic_slice_in_dim(x, (here ^ mask) * width, width, axis=split)
+        if mask:
+            part = lax.ppermute(part, axis, [(d, d ^ mask) for d in range(ways)])
+        full = lax.dynamic_update_slice_in_dim(full, part, (here ^ mask) * height, axis=join)
+    return full
 
 
 def padded_2(x, sides, width):
@@ -26,7 +42,7 @@
 
 
 def across_lines(values, local_step):
-    turned = lax.all_to_all(values, "gx", split_axis=3, concat_axis=2, tiled=True)
+    turned = swapped_with_each(values, "gx", 3, 2)
     return lax.all_to_all(local_step(turned), "gx", split_axis=2, concat_axis=3, tiled=True)
 
 

time: 1380 us -> 1320 us (0.957)
  blocking collectives: 439 us -> 313 us
  waiting for transfers between devices: 248 us -> 294 us
  starting transfers between devices: 26.9 us -> 68.4 us
    ppermute x0 -> x14, waiting for transfers between devices: none -> 117 us  [swapped_with_each(): part = lax.ppermute(part, axis, [(d, d ^ mask) for d in range(ways)])]
    all_to_all x1 -> x0, blocking collectives: 97.5 us -> none  [across_lines(): lax.all_to_all(values, 'gx', split_axis=3, concat_axis=2, tiled=True)]
    all_to_all x1, waiting for transfers between devices: 117 us -> 47.4 us  [depth_lines(): lax.all_to_all(local_step(turned), 'gz', split_axis=1, concat_axis=3, til...]
    all_to_all x2 -> x1, blocking collectives: 102 us -> 50.9 us  [depth_lines(): lax.all_to_all(local_step(turned), 'gz', split_axis=1, concat_axis=3, til...]
    all_to_all x4 -> x0, local copies, waits for them, and re-layouts: 26.3 us -> none  [across_lines(): lax.all_to_all(values, 'gx', split_axis=3, concat_axis=2, tiled=True)]
    ppermute x0 -> x14, starting transfers between devices: none -> 24.9 us  [swapped_with_each(): part = lax.ppermute(part, axis, [(d, d ^ mask) for d in range(ways)])]
    all_to_all x1, blocking collectives: 97.9 us -> 121 us  [across_lines(): lax.all_to_all(local_step(turned), 'gx', split_axis=2, concat_axis=3, til...]
    all_to_all x1, starting transfers between devices: 4.68 us -> 22.4 us  [across_lines(): lax.all_to_all(local_step(turned), 'gx', split_axis=2, concat_axis=3, til...]
  transfers between devices with their start and end apart: 12 -> 26, of which waited for: 6 -> 16; matrix products, arithmetic and copies ran while one was open for 2% -> 3% of each run, Pallas kernels for 0% -> 0%
where the time goes in v1:
time: 1320 us; the launch traced here: 1310 us
  other arithmetic  372 us (28%)
  blocking collectives  313 us (24%)
  waiting for transfers between devices  294 us (22%)
  local copies, waits for them, and re-layouts  206 us (16%)
  starting transfers between devices  68.4 us (5%)
  matrix products  43.1 us (3%)
  between operations  14.8 us (1%)
    another operation x3, other arithmetic, local(): jnp.stack([back_g + spread_back, back_m * growth]).astype(jnp.bfloat16)  197 us
    all_to_all x1, blocking collectives, across_lines(): lax.all_to_all(local_step(turned), 'gx', split_axis=2, concat_axis=3, til...  121 us
    add x1, other arithmetic, coupling_forward(): return (scale, growth, magnetic_f * growth + pre_shift)  119 us
    ppermute x14, waiting for transfers between devices, swapped_with_each(): part = lax.ppermute(part, axis, [(d, d ^ mask) for d in range(ways)])  117 us
    all_to_all x2, blocking collectives, depth_lines(): lax.all_to_all(values, 'gz', split_axis=3, concat_axis=1, tiled=True)  108 us
    all_to_all x1, waiting for transfers between devices, across_lines(): lax.all_to_all(local_step(turned), 'gx', split_axis=2, concat_axis=3, til...  89.8 us
    all_to_all x1, blocking collectives, depth_lines(): lax.all_to_all(local_step(turned), 'gz', split_axis=1, concat_axis=3, til...  50.9 us
    unnamed x35, local copies, waits for them, and re-layouts  48.6 us
  transfers between devices with their start and end apart: 26, of which 16 were waited for; matrix products, arithmetic and copies ran while one was open for 3% of the time, Pallas kernels for 0%

profile of v1, /device:TPU:0, one launch (start us, length us, event | category | flops | bytes accessed | tf_op | source)
XLA Modules:
  0.0 1311.3 jit_solution(2802043343012531742)
XLA Ops:
  7.2 33.2 %all_gather.6 = bf16[512,512]{1,0:T(8,128)(2,1)S(1)} all-gather(bf16[64,512]{1,0:T(8,128)(2,1)} %param.9), channel_id=1, replica_groups=mesh['gx'=8,'gz'=4] {'gx'}, dimensions={0}, use_global_device_ids=true | all-gather | bytes 589824 | tf_op jit(solution)/shard_map/all_gather | solution.py:88
  41.2 7.8 fusion.77
  49.0 7.9 copy.75
  56.8 53.8 %all_to_all.105 = bf16[2,16,128,512]{2,1,0,3:T(8,128)(2,1)} all-to-all(bf16[2,16,128,512]{2,1,0,3:T(8,128)(2,1)} %copy.75), channel_id=1, replica_groups=mesh['gx'=8,'gz'=4] {'gz'}, dimensions={3} | all-to-all | bytes 8388608 | tf_op jit(solution)/shard_map/all_to_all | solution.py:40
  110.7 9.0 copy.76
  133.5 47.4 %all-to-all-done.1 = bf16[2,64,128,128]{3,2,0,1:T(8,128)(2,1)} async-done(((bf16[2,64,128,128]{3,2,0,1:T(8,128)(2,1)}), bf16[2,64,128,128]{3,2,0,1:T(8,128)(2,1)}, u32[]{:S(2)}, u32[]{:S(2)}) %all-to-all-start.1) | async-done | bytes 4194336 | tf_op jit(solution)/shard_map/all_to_all | solution.py:41
  211.4 20.2 %collective-permute-done.1 = bf16[2,16,128,64]{2,3,1,0:T(8,128)(2,1)S(1)} collective-permute-done((bf16[2,16,128,64]{2,3,1,0:T(8,128)(2,1)}, bf16[2,16,128,64]{2,3,1,0:T(8,128)(2,1)S(1)}, u32[]{:S(2)}, u32[]{:S(2)}) %collective-permute-start.1) | collective-permute-done | bytes 524320 | tf_op jit(solution)/shard_map/ppermute | solution.py:21
  241.9 28.6 %collective-permute-done.4 = bf16[2,16,128,64]{2,3,1,0:T(8,128)(2,1)S(1)} collective-permute-done((bf16[2,16,128,64]{2,3,1,0:T(8,128)(2,1)}, bf16[2,16,128,64]{2,3,1,0:T(8,128)(2,1)S(1)}, u32[]{:S(2)}, u32[]{:S(2)}) %collective-permute-start.4) | collective-permute-done | bytes 524320 | tf_op jit(solution)/shard_map/ppermute | solution.py:21
  273.0 9.4 convert_bitcast_fusion.2
  282.4 12.9 copy.79
  295.3 10.6 reshape.38
  305.9 22.4 %all-to-all-start.2 = ((bf16[8,2,131072]{2,1,0:T(2,128)(2,1)}), bf16[8,2,131072]{2,1,0:T(2,128)(2,1)}, u32[]{:S(2)}, u32[]{:S(2)}) async-start(bf16[8,2,131072]{2,1,0:T(2,128)(2,1)} %reshape.38), calls=%async_computation.2 | async-start | bytes 8388608 | tf_op jit(solution)/shard_map/all_to_all | solution.py:46
  331.0 89.8 %all-to-all-done.2 = bf16[8,2,131072]{2,1,0:T(2,128)(2,1)} async-done(((bf16[8,2,131072]{2,1,0:T(2,128)(2,1)}), bf16[8,2,131072]{2,1,0:T(2,128)(2,1)}, u32[]{:S(2)}, u32[]{:S(2)}) %all-to-all-start.2) | async-done | bytes 4194336 | tf_op jit(solution)/shard_map/all_to_all | solution.py:46
  420.7 10.3 reshape.39
  431.0 9.3 copy.111
  473.3 11.1 fusion.10
  484.4 118.6 %add_add_fusion = (bf16[16,128,512]{1,2,0:T(8,128)(2,1)S(1)}, f32[16,128,512]{1,2,0:T(8,128)}) fusion(f32[16,128,512]{1,2,0:T(8,128)} %bitcast.151, f32[18,130,514]{1,2,0:T(8,128)} %fusion.10, f32[]{:T(128)} %bitcast.74, f32[]{:T(128)} %bitcast.73, f32[]{:T(128)} %bitcast.72, f32[]{:T(128)} %bitcast.71, f32[]{:T(128)} %bitcast.70, f32[]{:T(128)} %bitcast.69, ...), kind=kLoop, calls=%fused_computation.163 | loop fusion | flops 114294784 | bytes 123732184 | tf_op jit(solution)/shard_map/add | solution.py:82
  608.9 35.3 %all-reduce.4.cloned.1.call-done = f32[2,128,512]{2,1,0:T(8,128)} async-done(((f32[2,128,512]{2,1,0:T(8,128)}), f32[2,128,512]{2,1,0:T(8,128)}) %all-reduce.4.cloned.1.call-update) | async-done | bytes 524304 | tf_op jit(solution)/shard_map/psum | solution.py:127
  686.7 22.6 %fusion.1 = f32[2,18,130,514]{2,3,1,0:T(8,128)S(1)} fusion(bf16[2,1,130,512]{2,3,1,0:T(8,128)(2,1)} %collective-permute-done.14, bf16[2,1,130,512]{2,3,1,0:T(8,128)(2,1)S(1)} %collective-permute-done.13, bf16[2,16,1,512]{2,3,1,0:T(8,128)(2,1)} %copy.93, bf16[2,16,1,512]{2,3,1,0:T(8,128)(2,1)} %copy.92, bf16[1,16,128,512]{2,3,1,0:T(8,128)(2,1)S(1)} %multiply_convert_fusion, ...), kind=kLoop, calls=%fused_computation.8 | loop fusion | flops 50515920 | bytes 14414400 | tf_op jit(solution)/shard_map/convert_element_type | solution.py:135
  716.2 196.3 %fusion.84 = bf16[1,16,128,512]{2,3,1,0:T(8,128)(2,1)S(1)} fusion(f32[18,130,514]{1,2,0:T(8,128)} %get-tuple-element.5, f32[]{:T(128)} %bitcast.74, f32[]{:T(128)} %bitcast.73, f32[]{:T(128)} %bitcast.72, f32[]{:T(128)} %bitcast.71, f32[]{:T(128)} %bitcast.70, f32[]{:T(128)} %bitcast.69, f32[]{:T(128)} %bitcast.68, f32[]{:T(128)} %bitcast.67, f32[]{:T(128)} %bitcast.66, ...), kind=kLoop, calls=%fused_computation.176 | loop fusion | flops 115343360 | bytes 228852000 | tf_op jit(solution)/shard_map/stack | solution.py:140
  928.4 19.1 %collective-permute-done.16 = bf16[2,16,128,64]{2,3,1,0:T(8,128)(2,1)S(1)} collective-permute-done((bf16[2,16,128,64]{2,3,1,0:T(8,128)(2,1)S(1)}, bf16[2,16,128,64]{2,3,1,0:T(8,128)(2,1)S(1)}, u32[]{:S(2)}, u32[]{:S(2)}) %collective-permute-start.16) | collective-permute-done | bytes 524320 | tf_op jit(solution)/shard_map/ppermute | solution.py:21
  959.0 14.0 %collective-permute-done.20 = bf16[2,16,128,64]{2,3,1,0:T(8,128)(2,1)S(1)} collective-permute-done((bf16[2,16,128,64]{2,3,1,0:T(8,128)(2,1)S(1)}, bf16[2,16,128,64]{2,3,1,0:T(8,128)(2,1)S(1)}, u32[]{:S(2)}, u32[]{:S(2)}) %collective-permute-start.20) | collective-permute-done | bytes 524320 | tf_op jit(solution)/shard_map/ppermute | solution.py:21
  973.1 11.0 collective-permute-done.21
  990.5 13.3 %copy.94 = bf16[2,16,1024,64]{3,1,0,2:T(8,128)(2,1)} copy(bf16[2,16,1024,64]{2,3,1,0:T(8,128)(2,1)} %convert_bitcast_fusion.1) | data formatting | bytes 8388608 | tf_op jit(solution)/shard_map/convert_element_type | solution.py:109
  1003.8 10.5 reshape.40
  1014.3 121.4 %all_to_all.106 = bf16[8,2,131072]{2,1,0:T(2,128)(2,1)} all-to-all(bf16[8,2,131072]{2,1,0:T(2,128)(2,1)} %reshape.40), channel_id=1, replica_groups=mesh['gx'=8,'gz'=4] {'gx'}, dimensions={0} | all-to-all | bytes 8388608 | tf_op jit(solution)/shard_map/all_to_all | solution.py:46
  1135.7 10.3 reshape.41
  1146.0 14.8 %copy.114 = bf16[2,16,128,8,64]{2,1,0,4,3:T(8,128)(2,1)} copy(bf16[2,16,128,8,64]{4,1,0,2,3:T(8,128)(2,1)} %bitcast.156) | data formatting | bytes 8388608 | tf_op jit(solution)/shard_map/all_to_all | solution.py:46
  1160.8 53.8 %all_to_all.107 = bf16[2,16,128,512]{2,1,0,3:T(8,128)(2,1)} all-to-all(bf16[2,16,128,512]{2,1,0,3:T(8,128)(2,1)} %bitcast.158), channel_id=1, replica_groups=mesh['gx'=8,'gz'=4] {'gz'}, dimensions={3} | all-to-all | bytes 8388608 | tf_op jit(solution)/shard_map/all_to_all | solution.py:40
  1214.6 9.0 copy.99
  1229.8 50.9 %all_to_all.108 = bf16[2,64,128,128]{3,2,0,1:T(8,128)(2,1)S(1)} all-to-all(bf16[2,64,128,128]{3,2,0,1:T(8,128)(2,1)S(1)} %copy.101), channel_id=1, replica_groups=mesh['gx'=8,'gz'=4] {'gz'}, dimensions={1} | all-to-all | bytes 8388608 | tf_op jit(solution)/shard_map/all_to_all | solution.py:41
  1293.9 10.4 convolution_add_fusion
  (138 shorter events, 201.6 us)
Async XLA Ops:
  7.2 112.5 %copy-start = (bf16[64,64]{1,0:T(8,128)(2,1)S(1)}, bf16[64,64]{1,0:T(8,128)(2,1)}, u32[]{:S(2)}) copy-start(bf16[64,64]{1,0:T(8,128)(2,1)} %param.10) | copy-start | bytes 24580
  127.8 53.1 %all-to-all-start.1 = ((bf16[2,64,128,128]{3,2,0,1:T(8,128)(2,1)}), bf16[2,64,128,128]{3,2,0,1:T(8,128)(2,1)}, u32[]{:S(2)}, u32[]{:S(2)}) async-start(bf16[2,64,128,128]{3,2,0,1:T(8,128)(2,1)} %copy.77), calls=%async_computation.1 | async-start | bytes 8388608 | tf_op jit(solution)/shard_map/all_to_all | solution.py:41
  132.7 140.3 %all-gather.2.cloned.1.call-start = ((), (), s32[]{:S(2)}) async-start(), calls=%async_computation.6 | async-start | bytes 2359296 | tf_op jit(solution)/shard_map/all_gather | solution.py:87
  193.7 13.7 %collective-permute-start = (bf16[2,16,128,64]{2,3,1,0:T(8,128)(2,1)}, bf16[2,16,128,64]{2,3,1,0:T(8,128)(2,1)S(1)}, u32[]{:S(2)}, u32[]{:S(2)}) collective-permute-start(bf16[2,16,128,64]{2,3,1,0:T(8,128)(2,1)} %get-tuple-element.30), channel_id=1, source_target_pairs={{0,4},{4,0},{8,12},{12,8},{16,20},{20,16},{24,28},{28,24},{1,5},{5... | collective-permute-start | bytes 1572872 | tf_op jit(solution)/shard_map/ppermute | solution.py:21
  195.4 36.2 %collective-permute-start.1 = (bf16[2,16,128,64]{2,3,1,0:T(8,128)(2,1)}, bf16[2,16,128,64]{2,3,1,0:T(8,128)(2,1)S(1)}, u32[]{:S(2)}, u32[]{:S(2)}) collective-permute-start(bf16[2,16,128,64]{2,3,1,0:T(8,128)(2,1)} %get-tuple-element.29), channel_id=1, source_target_pairs={{0,8},{4,12},{8,0},{12,4},{16,24},{20,28},{24,16},{28,20},{1,9},{5... | collective-permute-start | bytes 1572872 | tf_op jit(solution)/shard_map/ppermute | solution.py:21
  195.4 44.8 %collective-permute-start.2 = (bf16[2,16,128,64]{2,3,1,0:T(8,128)(2,1)}, bf16[2,16,128,64]{2,3,1,0:T(8,128)(2,1)S(1)}, u32[]{:S(2)}, u32[]{:S(2)}) collective-permute-start(bf16[2,16,128,64]{2,3,1,0:T(8,128)(2,1)} %get-tuple-element.28), channel_id=1, source_target_pairs={{0,12},{4,8},{8,4},{12,0},{16,28},{20,24},{24,20},{28,16},{1,13},{... | collective-permute-start | bytes 1572872 | tf_op jit(solution)/shard_map/ppermute | solution.py:21
  197.2 43.8 %collective-permute-start.3 = (bf16[2,16,128,64]{2,3,1,0:T(8,128)(2,1)}, bf16[2,16,128,64]{2,3,1,0:T(8,128)(2,1)S(1)}, u32[]{:S(2)}, u32[]{:S(2)}) collective-permute-start(bf16[2,16,128,64]{2,3,1,0:T(8,128)(2,1)} %get-tuple-element.27), channel_id=1, source_target_pairs={{0,16},{4,20},{8,24},{12,28},{16,0},{20,4},{24,8},{28,12},{1,17},{... | collective-permute-start | bytes 1572872 | tf_op jit(solution)/shard_map/ppermute | solution.py:21
  199.2 71.2 %collective-permute-start.4 = (bf16[2,16,128,64]{2,3,1,0:T(8,128)(2,1)}, bf16[2,16,128,64]{2,3,1,0:T(8,128)(2,1)S(1)}, u32[]{:S(2)}, u32[]{:S(2)}) collective-permute-start(bf16[2,16,128,64]{2,3,1,0:T(8,128)(2,1)} %get-tuple-element.26), channel_id=1, source_target_pairs={{0,20},{4,16},{8,28},{12,24},{16,4},{20,0},{24,12},{28,8},{1,21},{... | collective-permute-start | bytes 1572872 | tf_op jit(solution)/shard_map/ppermute | solution.py:21
  207.4 63.9 %collective-permute-start.5 = (bf16[2,16,128,64]{2,3,1,0:T(8,128)(2,1)}, bf16[2,16,128,64]{2,3,1,0:T(8,128)(2,1)S(1)}, u32[]{:S(2)}, u32[]{:S(2)}) collective-permute-start(bf16[2,16,128,64]{2,3,1,0:T(8,128)(2,1)} %get-tuple-element.25), channel_id=1, source_target_pairs={{0,24},{4,28},{8,16},{12,20},{16,8},{20,12},{24,0},{28,4},{1,25},{... | collective-permute-start | bytes 1572872 | tf_op jit(solution)/shard_map/ppermute | solution.py:21
  231.6 40.6 %collective-permute-start.6 = (bf16[2,16,128,64]{2,3,1,0:T(8,128)(2,1)S(1)}, bf16[2,16,128,64]{2,3,1,0:T(8,128)(2,1)S(1)}, u32[]{:S(2)}, u32[]{:S(2)}) collective-permute-start(bf16[2,16,128,64]{2,3,1,0:T(8,128)(2,1)S(1)} %get-tuple-element.24), channel_id=1, source_target_pairs={{0,28},{4,24},{8,20},{12,16},{16,12},{20,8},{24,4},{28,0},{1,29},{... | collective-permute-start | bytes 1572872 | tf_op jit(solution)/shard_map/ppermute | solution.py:21
  305.9 23.0 %copy-start.13 = (f32[2,3,3,3]{3,0,2,1:T(2,128)S(1)}, f32[2,3,3,3]{3,0,2,1:T(2,128)}, u32[]{:S(2)}) copy-start(f32[2,3,3,3]{3,0,2,1:T(2,128)} %param.11) | copy-start | bytes 652
  305.9 114.8 %all-to-all-start.2 = ((bf16[8,2,131072]{2,1,0:T(2,128)(2,1)}), bf16[8,2,131072]{2,1,0:T(2,128)(2,1)}, u32[]{:S(2)}, u32[]{:S(2)}) async-start(bf16[8,2,131072]{2,1,0:T(2,128)(2,1)} %reshape.38), calls=%async_computation.2 | async-start | bytes 8388608 | tf_op jit(solution)/shard_map/all_to_all | solution.py:46
  328.3 316.0 %all-reduce.4.cloned.1.call-start = ((), (), s32[]{:S(2)}) async-start(), calls=%async_computation.7 | async-start | bytes 1048576 | tf_op jit(solution)/shard_map/psum | solution.py:127
  450.5 9.2 collective-permute-start.7
  454.7 6.8 collective-permute-start.8
  463.4 6.5 copy-start.5
  464.9 7.7 collective-permute-start.10
  466.4 6.3 collective-permute-start.9
  603.0 41.2 %copy-start.12 = (f32[2,128,512]{2,1,0:T(8,128)S(1)}, f32[2,128,512]{2,1,0:T(8,128)}, u32[]{:S(2)}) copy-start(f32[2,128,512]{2,1,0:T(8,128)} %param.7) | copy-start | bytes 1572868
  661.3 8.6 collective-permute-start.11
  668.6 5.8 collective-permute-start.12
  680.5 3.0 collective-permute-start.13
  681.8 4.9 collective-permute-start.14
  914.8 9.6 collective-permute-start.15
  917.2 30.3 %collective-permute-start.16 = (bf16[2,16,128,64]{2,3,1,0:T(8,128)(2,1)S(1)}, bf16[2,16,128,64]{2,3,1,0:T(8,128)(2,1)S(1)}, u32[]{:S(2)}, u32[]{:S(2)}) collective-permute-start(bf16[2,16,128,64]{2,3,1,0:T(8,128)(2,1)S(1)} %get-tuple-element.15), channel_id=1, source_target_pairs={{0,8},{4,12},{8,0},{12,4},{16,24},{20,28},{24,16},{28,20},{1,9},{5... | collective-permute-start | bytes 1572872 | tf_op jit(solution)/shard_map/ppermute | solution.py:21
  918.7 38.0 %collective-permute-start.17 = (bf16[2,16,128,64]{2,3,1,0:T(8,128)(2,1)S(1)}, bf16[2,16,128,64]{2,3,1,0:T(8,128)(2,1)S(1)}, u32[]{:S(2)}, u32[]{:S(2)}) collective-permute-start(bf16[2,16,128,64]{2,3,1,0:T(8,128)(2,1)S(1)} %get-tuple-element.16), channel_id=1, source_target_pairs={{0,12},{4,8},{8,4},{12,0},{16,28},{20,24},{24,20},{28,16},{1,13},{... | collective-permute-start | bytes 1572872 | tf_op jit(solution)/shard_map/ppermute | solution.py:21
  918.9 65.4 %copy-start.14 = (bf16[1024,1024]{1,0:T(8,128)(2,1)S(1)}, bf16[1024,1024]{1,0:T(8,128)(2,1)}, u32[]{:S(2)}) copy-start(bf16[1024,1024]{1,0:T(8,128)(2,1)} %all-gather.2.cloned.1.call-done) | copy-start | bytes 6291460
  918.9 38.0 %collective-permute-start.18 = (bf16[2,16,128,64]{2,3,1,0:T(8,128)(2,1)S(1)}, bf16[2,16,128,64]{2,3,1,0:T(8,128)(2,1)S(1)}, u32[]{:S(2)}, u32[]{:S(2)}) collective-permute-start(bf16[2,16,128,64]{2,3,1,0:T(8,128)(2,1)S(1)} %get-tuple-element.18), channel_id=1, source_target_pairs={{0,16},{4,20},{8,24},{12,28},{16,0},{20,4},{24,8},{28,12},{1,17},{... | collective-permute-start | bytes 1572872 | tf_op jit(solution)/shard_map/ppermute | solution.py:21
  921.9 37.0 %collective-permute-start.19 = (bf16[2,16,128,64]{2,3,1,0:T(8,128)(2,1)S(1)}, bf16[2,16,128,64]{2,3,1,0:T(8,128)(2,1)S(1)}, u32[]{:S(2)}, u32[]{:S(2)}) collective-permute-start(bf16[2,16,128,64]{2,3,1,0:T(8,128)(2,1)S(1)} %get-tuple-element.19), channel_id=1, source_target_pairs={{0,20},{4,16},{8,28},{12,24},{16,4},{20,0},{24,12},{28,8},{1,21},{... | collective-permute-start | bytes 1572872 | tf_op jit(solution)/shard_map/ppermute | solution.py:21
  924.4 48.6 %collective-permute-start.20 = (bf16[2,16,128,64]{2,3,1,0:T(8,128)(2,1)S(1)}, bf16[2,16,128,64]{2,3,1,0:T(8,128)(2,1)S(1)}, u32[]{:S(2)}, u32[]{:S(2)}) collective-permute-start(bf16[2,16,128,64]{2,3,1,0:T(8,128)(2,1)S(1)} %get-tuple-element.17), channel_id=1, source_target_pairs={{0,24},{4,28},{8,16},{12,20},{16,8},{20,12},{24,0},{28,4},{1,25},{... | collective-permute-start | bytes 1572872 | tf_op jit(solution)/shard_map/ppermute | solution.py:21
  947.5 36.6 %collective-permute-start.21 = (bf16[2,16,128,64]{2,3,1,0:T(8,128)(2,1)S(1)}, bf16[2,16,128,64]{2,3,1,0:T(8,128)(2,1)S(1)}, u32[]{:S(2)}, u32[]{:S(2)}) collective-permute-start(bf16[2,16,128,64]{2,3,1,0:T(8,128)(2,1)S(1)} %get-tuple-element.12), channel_id=1, source_target_pairs={{0,28},{4,24},{8,20},{12,16},{16,12},{20,8},{24,4},{28,0},{1,29},{... | collective-permute-start | bytes 1572872 | tf_op jit(solution)/shard_map/ppermute | solution.py:21
  1286.6 7.3 copy-start.9
  (9 other events, 24.2 us)
Sparse Core Ops, SparseCore 0:
  135.7 50.8 all-gather.1
  609.0 35.1 all-reduce.3
